TPU v7x, 128 devices: a whole 4x4x4 slice. The times are simulated.
128 devices in a mesh: section: 2 (over x_lo), rows: 8 (over y, x_hi), chan: 8 (over z, core).
Axes of the slice: x: 4 (x_hi: 2, x_lo: 2; x = x_hi * 2 + x_lo), y: 4, z: 4, core: 2. Of those that a mesh axis runs over, the one named last changes fastest.
Arguments:
- condition: float32 [12, 128, 1024], P(None, 'rows'), may hold values from -6 to 6
- target: float32 [12, 128, 1024], P(None, 'rows'), may hold values from -6 to 6
- noise_draw: float32 [12, 128, 1024], P(None, 'rows'), may hold values from -6 to 6
- sigma_index: int32 [1], replicated, may hold values from 0 to 31
- reg_first: bfloat16 [3, 3, 12, 128], P(None, None, None, 'chan'), may hold values from -0.625 to 0.625
- reg_second: bfloat16 [3, 3, 128, 12], P(None, None, 'chan'), may hold values from -0.1875 to 0.1875
- first_kernel: bfloat16 [3, 3, 24, 128], P(None, None, None, ('section', 'chan')), may hold values from -0.4375 to 0.4375
- second_kernel: bfloat16 [3, 3, 128, 128], P(None, None, None, ('section', 'chan')), may hold values from -0.1875 to 0.1875
- third_kernel: bfloat16 [3, 3, 128, 12], P(None, None, ('section', 'chan')), may hold values from -0.1875 to 0.1875
- film_scale: bfloat16 [128], P(('section', 'chan')), may hold values from -4 to 4
Outputs:
- denoised: bfloat16 [12, 128, 1024], P(None, 'rows')
- grad_first: float32 [3, 3, 24, 128], P(None, None, None, ('section', 'chan'))
- grad_second: float32 [3, 3, 128, 128], P(None, None, None, ('section', 'chan'))
- grad_third: float32 [3, 3, 128, 12], P(None, None, ('section', 'chan'))
- grad_film: float32 [128], P(('section', 'chan'))
Inputs may be any that keep to these rules, and one draw needn't show every extreme that they name: `sigma_index`: an index into the table of 32 noise levels.
All inputs are finite; a program needn't handle non-finite values.
Results may differ from a plain program's by a relative error of at most 0.008.
Values may be sent and summed in bfloat16 or wider, within the bound.
No kernel may reach another device: no remote copies, remote signals or barrier semaphores. Data moves between devices by JAX's collectives and lax.ppermute only.
A program may use at most 128 MiB of HBM per device.

v0:
```python
import math
import jax
import jax.numpy as jnp
from jax import lax
from jax.sharding import PartitionSpec as P

COUT = 12
NSIG = 32
sigma_low = 0.25
sigma_high = 4.0
rho_power = 7.0
sigma_data = 0.5


def padded(array, sides, width):
    for axis, dim in sides:
        size, length = (lax.axis_size(axis), array.shape[dim])
        up = [(i, (i + 1) % size) for i in range(size - 1)]
        down = [(j, i) for i, j in up]
        last = lax.slice_in_dim(array, length - width, length, axis=dim)
        leading = lax.slice_in_dim(array, 0, width, axis=dim)
        before = lax.ppermute(last, axis, up)
        after = lax.ppermute(leading, axis, down)
        array = jnp.concatenate([before, array, after], axis=dim)
    return array


def noise_terms(sigma_index):
    steps_at = jnp.arange(NSIG, dtype=jnp.float32) / (NSIG - 1)
    high_root = sigma_high ** (1.0 / rho_power)
    low_root = sigma_low ** (1.0 / rho_power)
    levels = (high_root + steps_at * (low_root - high_root)) ** rho_power
    picked = jnp.arange(NSIG, dtype=jnp.int32) == sigma_index[0]
    sigma_level = jnp.sum(jnp.where(picked, levels, jnp.zeros_like(levels)))
    total_var = sigma_level * sigma_level + sigma_data * sigma_data
    skip_coef = sigma_data * sigma_data / total_var
    out_coef = sigma_level * sigma_data / jnp.sqrt(total_var)
    in_coef = 1.0 / jnp.sqrt(total_var)
    noise_coef = jnp.log(8.0 * sigma_level) / 4.0
    loss_weight = total_var / (sigma_level * sigma_data) ** 2
    return (sigma_level, skip_coef, out_coef, in_coef, noise_coef, loss_weight)


def conv_rows(grid_field, kernel):
    result_conv = lax.conv_general_dilated(
        grid_field[None],
        kernel,
        (1, 1),
        ((0, 0), (1, 1)),
        dimension_numbers=("NCHW", "HWIO", "NCHW"),
        preferred_element_type=jnp.float32,
    )
    return result_conv[0]


def kernel_grad(grid_field, delta_in):
    result_conv = lax.conv_general_dilated(
        grid_field[:, None],
        delta_in[:, None],
        (1, 1),
        ((0, 0), (1, 1)),
        dimension_numbers=("NCHW", "OIHW", "NCHW"),
        preferred_element_type=jnp.float32,
    )
    return jnp.transpose(result_conv, (2, 3, 0, 1))


def turned(kernel):
    return jnp.transpose(jnp.flip(kernel, (0, 1)), (0, 1, 3, 2))


def silu_slope(pre_act):
    sigmoid_at = jax.nn.sigmoid(pre_act)
    return sigmoid_at * (1.0 + pre_act * (1.0 - sigmoid_at))


def grid_rows(grid_field, first_row, total_rows):
    places = first_row + jnp.arange(grid_field.shape[1], dtype=jnp.int32)
    inside = (places >= 0) & (places < total_rows)
    return jnp.where(inside[None, :, None], grid_field, jnp.zeros_like(grid_field))


def shards(
    condition,
    target,
    noise_draw,
    sigma_index,
    reg_first,
    reg_second,
    first_kernel,
    second_kernel,
    third_kernel,
    film_scale,
):
    rows_dev = condition.shape[1]
    grid_width = condition.shape[2]
    total_rows = rows_dev * lax.axis_size("rows")
    slab_start = lax.axis_index("rows") * rows_dev
    section_id = lax.axis_index("section")
    member = lax.axis_index(("section", "chan"))
    local_ch = film_scale.shape[0]
    sigma_level, skip_coef, out_coef, in_coef, noise_coef, loss_weight = noise_terms(sigma_index)
    grad_scale = 1.0 / math.sqrt(COUT * total_rows * grid_width)
    cond_low = condition.astype(jnp.bfloat16)
    cond_rim = padded(cond_low, (("rows", 1),), 2)
    half_rows = rows_dev // lax.axis_size("section")
    half_start = section_id * half_rows
    reg_input = lax.dynamic_slice_in_dim(cond_rim, half_start, half_rows + 4, 1)
    reg_hidden = jax.nn.silu(conv_rows(reg_input, reg_first))
    reg_hidden = grid_rows(reg_hidden, slab_start + half_start - 1, total_rows).astype(jnp.bfloat16)
    mean_part = conv_rows(reg_hidden, reg_second)
    mean_half = lax.psum(mean_part, "chan").astype(jnp.bfloat16)
    mean_field = lax.all_gather(mean_half, "section", axis=1, tiled=True)
    resid_field = target - mean_field.astype(jnp.float32)
    noisy_field = resid_field + sigma_level * noise_draw
    scaled_in = (in_coef * noisy_field).astype(jnp.bfloat16)
    film_gain = 1.0 + noise_coef * film_scale.astype(jnp.float32)
    input_rim = padded(scaled_in, (("rows", 1),), 2)
    stacked = jnp.concatenate([input_rim, cond_rim], 0)
    whole_first, whole_film = (
        lax.all_gather(first_kernel, ("section", "chan"), axis=3, tiled=True),
        lax.all_gather(film_scale, ("section", "chan"), axis=0, tiled=True),
    )
    first_all = conv_rows(stacked, whole_first)
    gain_all = (1.0 + noise_coef * whole_film.astype(jnp.float32))[:, None, None]
    hidden_full = grid_rows(jax.nn.silu(first_all * gain_all), slab_start - 1, total_rows).astype(
        jnp.bfloat16
    )
    first_mine = lax.dynamic_slice_in_dim(first_all, member * local_ch, local_ch, 0)[:, 1:-1]
    second_act = conv_rows(hidden_full, second_kernel)
    second_hidden = jax.nn.silu(second_act).astype(jnp.bfloat16)
    second_rim = padded(second_hidden, (("rows", 1),), 1)
    out_part = conv_rows(second_rim, third_kernel)
    out_full = lax.psum(out_part, ("section", "chan"))
    den_value = skip_coef * noisy_field + out_coef * out_full
    out_delta = (2.0 * loss_weight * out_coef * grad_scale * (den_value - resid_field)).astype(
        jnp.bfloat16
    )
    out_delta_rim = padded(out_delta, (("rows", 1),), 1)
    grad_third = kernel_grad(second_rim, out_delta)
    second_delta = (conv_rows(out_delta_rim, turned(third_kernel)) * silu_slope(second_act)).astype(
        jnp.bfloat16
    )
    second_delta_rim = padded(second_delta, (("rows", 1),), 1)
    grad_second = kernel_grad(hidden_full, second_delta)
    whole_second = lax.all_gather(second_kernel, ("section", "chan"), axis=3, tiled=True)
    mine_second = turned(lax.dynamic_slice_in_dim(whole_second, member * local_ch, local_ch, 2))
    empty_sum = jnp.zeros((local_ch, rows_dev, grid_width), jnp.float32)
    shard_part = lax.all_gather(second_delta_rim, ("section", "chan"), axis=0, tiled=True)
    kernel_part = lax.slice_in_dim(mine_second, 0, shard_part.shape[0], axis=2)
    back_first = empty_sum + conv_rows(shard_part, kernel_part)
    gain_mine = film_gain[:, None, None]
    first_grad = back_first * silu_slope(first_mine * gain_mine)
    grad_film = noise_coef * jnp.sum(first_grad * first_mine, axis=(1, 2))
    first_delta = (first_grad * gain_mine).astype(jnp.bfloat16)
    grad_first = kernel_grad(stacked[:, 1:-1], first_delta)
    grad_parts = (grad_first, grad_second, grad_third, grad_film)
    den_out = den_value.astype(jnp.bfloat16)
    grad_first, grad_second, grad_third, grad_film = lax.psum(
        (grad_parts[0], grad_parts[1], grad_parts[2], grad_parts[3]), "rows"
    )
    return (den_out, grad_first, grad_second, grad_third, grad_film)


def solution(mesh):
    return jax.shard_map(
        shards,
        mesh=mesh,
        in_specs=(
            P(None, "rows", None),
            P(None, "rows", None),
            P(None, "rows", None),
            P(),
            P(None, None, None, "chan"),
            P(None, None, "chan", None),
            P(None, None, None, ("section", "chan")),
            P(None, None, None, ("section", "chan")),
            P(None, None, ("section", "chan"), None),
            P(("section", "chan")),
        ),
        out_specs=(
            P(None, "rows", None),
            P(None, None, None, ("section", "chan")),
            P(None, None, None, ("section", "chan")),
            P(None, None, ("section", "chan"), None),
            P(("section", "chan")),
        ),
        check_vma=False,
    )
```

profile of v0, /device:TPU:0, one launch (start us, length us, event | category | flops | bytes accessed | tf_op | source)
XLA Modules:
  0.0 844.1 jit_solution(11145103124998721474)
XLA Ops:
  18.9 30.4 %all-reduce = bf16[128]{0:T(256)(128)(2,1)S(1)} all-reduce(bf16[128]{0:T(256)(128)(2,1)S(1)} %dynamic-update-slice), channel_id=1, replica_groups=mesh['section'=2,'rows'=8,'chan'=8] {'section','chan'}, use_global_device_ids=true, to_apply=%add | all-reduce | flops 128 | bytes 512
  58.5 7.3 select_bitcast_fusion.1
  75.3 27.6 %all-reduce.6 = bf16[12,8,1024]{2,1,0:T(8,128)(2,1)S(1)} all-reduce(f32[12,8,1024]{2,1,0:T(8,128)S(1)} %slice_bitcast_fusion.3), channel_id=1, replica_groups=mesh['section'=2,'rows'=8,'chan'=8] {'chan'}, use_global_device_ids=true, to_apply=%region_1.2 | all-reduce | flops 98304 | bytes 589824 | tf_op jit(solution)/shard_map/psum | solution.py:112
  112.7 7.0 collective-permute-start.2
  119.8 18.4 %all_gather.16 = bf16[3,3,24,128]{2,3,1,0:T(8,128)(2,1)S(1)} all-gather(bf16[3,3,24,8]{2,3,1,0:T(8,128)(2,1)S(1)} %copy-done.8), channel_id=1, replica_groups=mesh['section'=2,'rows'=8,'chan'=8] {'section','chan'}, dimensions={3}, use_global_device_ids=true | all-gather | bytes 58752 | tf_op jit(solution)/shard_map/all_gather | solution.py:121
  150.9 8.9 %broadcast_select_fusion = f32[18,8,129,128]{3,1,2,0:T(8,128)S(1)} fusion(pred[8,129]{0,1:T(8,128)(4,1)S(1)} %copy-done.10, bf16[3,3,24,128]{2,3,1,0:T(8,128)(2,1)S(1)} %all_gather.16, bf16[24,20,1,7,2]{0,3,4,1,2:T(8,128)(2,1)S(1)} %slice.71, bf16[24,20,1,8,129]{0,3,4,1,2:T(8,128)(2,1)} %copy.92), kind=kOutput, calls=%fused_computation.56 | convolution fusion | flops 1032574464 | bytes 10571400 | tf_op jit(solution)/shard_map/conv_general_dilated | solution.py:45
  163.7 12.6 %fusion.30 = f32[16,8,129,8]{3,1,2,0:T(8,128)} fusion(bf16[3,3,128,8]{2,3,1,0:T(8,128)(2,1)S(1)} %copy-done.9, bf16[18,1,7,1,128]{4,2,3,0,1:T(8,128)(2,1)S(1)} %get-tuple-element.17, bf16[18,1,7,1,128]{4,2,3,0,1:T(8,128)(2,1)S(1)} %get-tuple-element.16, bf16[18,1,8,129,128]{4,2,3,0,1:T(8,128)(2,1)S(1)} %select_bitcast_fusion), kind=kOutput, calls=%fused_computation.39 | convolution fusion | flops 328495104 | bytes 5366784 | tf_op jit(solution)/shard_map/conv_general_dilated | solution.py:45
  185.0 7.3 collective-permute-start.4
  192.3 18.4 %all_gather.19 = bf16[3,3,128,128]{2,3,1,0:T(8,128)(2,1)} all-gather(bf16[3,3,128,8]{2,3,1,0:T(8,128)(2,1)S(1)} %copy-done.9), channel_id=1, replica_groups=mesh['section'=2,'rows'=8,'chan'=8] {'section','chan'}, dimensions={3}, use_global_device_ids=true | all-gather | bytes 313344 | tf_op jit(solution)/shard_map/all_gather | solution.py:146
  211.5 18.9 %copy.120 = f32[18,8,129,128]{2,1,3,0:T(8,128)} copy(f32[18,8,129,128]{3,1,2,0:T(8,128)} %copy-done.2) | data formatting | bytes 19021824 | tf_op jit(solution)/shard_map/conv_general_dilated | solution.py:45
  230.4 17.9 %reshape.184 = f32[18,1,1032,128]{2,3,0,1:T(8,128)} reshape(f32[18,8,129,128]{2,1,3,0:T(8,128)} %copy.120) | data formatting | bytes 19021824 | tf_op jit(solution)/shard_map/conv_general_dilated | solution.py:45
  255.9 11.2 %broadcast_select_fusion.3 = f32[16,8,129,12]{3,1,2,0:T(8,128)} fusion(pred[8,129]{0,1:T(8,128)(4,1)S(1)} %copy-done.10, bf16[3,3,8,12]{3,2,1,0:T(8,128)(2,1)S(1)} %copy-done.13, bf16[8,18,1,7,2]{0,3,4,1,2:T(8,128)(2,1)S(1)} %slice.77, bf16[8,18,1,8,129]{0,3,4,1,2:T(8,128)(2,1)} %copy.95), kind=kOutput, calls=%fused_computation.59 | convolution fusion | flops 29636352 | bytes 1096584 | tf_op jit(solution)/shard_map/conv_general_dilated | solution.py:45
  267.0 8.0 copy.96
  278.2 8.4 %select_convert_fusion.1 = bf16[128,1,18,1024]{3,0,2,1:T(8,128)(2,1)} fusion(f32[128]{0:T(128)S(1)} %multiply_add_fusion.3, pred[18]{0:T(512)(128)(4,1)S(1)} %compare_and_fusion, f32[18,1,1032,128]{2,3,0,1:T(8,128)} %reshape.184), kind=kLoop, calls=%fused_computation.14 | loop fusion | flops 16515072 | bytes 14156306 | tf_op jit(solution)/shard_map/convert_element_type | solution.py:126
  287.3 111.4 %all-reduce.5.cloned.1.call-done = f32[12,16,1024]{2,1,0:T(8,128)} async-done(((f32[12,16,1024]{2,1,0:T(8,128)}), f32[12,16,1024]{2,1,0:T(8,128)}) %all-reduce.5.cloned.1.call-update) | async-done | bytes 786448 | tf_op jit(solution)/shard_map/psum | solution.py:134
  410.0 9.3 %slice.88 = f32[18,1,1024,128]{2,3,0,1:T(8,128)} slice(f32[18,1,1032,128]{2,3,0,1:T(8,128)} %reshape.184), slice={[0:18], [0:1], [0:1024], [0:128]} | slice | bytes 18874368 | tf_op jit(solution)/shard_map/conv_general_dilated | solution.py:45
  429.1 11.0 %broadcast_select_fusion.2 = f32[16,8,129,8]{3,1,2,0:T(8,128)} fusion(pred[8,129]{0,1:T(8,128)(4,1)S(1)} %copy-done.10, bf16[3,3,8,12]{3,2,1,0:T(8,128)(2,1)S(1)} %copy-done.13, bf16[12,18,1,7,2]{0,3,4,1,2:T(8,128)(2,1)S(1)} %slice.82, bf16[12,18,1,8,129]{0,3,4,1,2:T(8,128)(2,1)} %copy.99), kind=kOutput, calls=%fused_computation.58 | convolution fusion | flops 30023040 | bytes 983016 | tf_op jit(solution)/shard_map/conv_general_dilated | solution.py:45
  440.1 7.5 copy.100
  458.8 13.2 %copy.108 = bf16[24,1,18,1024]{0,1,3,2:T(2,128)(2,1)} copy(bf16[24,1,18,1024]{3,2,0,1:T(8,128)(2,1)S(1)} %slice_bitcast_fusion) | data formatting | bytes 1769472 | tf_op jit(solution)/shard_map/broadcast_in_dim | solution.py:58
  472.1 21.3 %copy.110 = bf16[128,1,18,1024]{0,1,3,2:T(2,128)(2,1)} copy(bf16[128,1,18,1024]{3,0,2,1:T(8,128)(2,1)} %select_convert_fusion.1) | data formatting | bytes 9437184 | tf_op jit(solution)/shard_map/convert_element_type | solution.py:126
  493.4 15.4 %copy.112 = bf16[8,1,18,1024]{0,1,3,2:T(2,128)(2,1)} copy(bf16[8,1,18,1024]{3,0,2,1:T(8,128)(2,1)S(1)} %copy-done.6) | data formatting | bytes 589824 | tf_op jit(solution)/shard_map/broadcast_in_dim | solution.py:58
  508.8 9.0 %copy.113 = bf16[12,1,16,1024]{0,1,3,2:T(2,128)(2,1)} copy(bf16[12,1,16,1024]{3,2,0,1:T(8,128)(2,1)S(1)} %bitcast.183) | data formatting | bytes 786432 | tf_op jit(solution)/shard_map/broadcast_in_dim | solution.py:59
  518.6 52.5 %fusion.140 = f32[3,3,8,12]{3,2,1,0:T(8,128)S(1)} fusion(bf16[8,1,18,1024]{0,1,3,2:T(2,128)(2,1)} %copy.112, bf16[12,1,16,1024]{0,1,3,2:T(2,128)(2,1)} %copy.113), kind=kOutput, calls=%fused_computation.171 | convolution fusion | flops 28293120 | bytes 691584 | tf_op jit(solution)/shard_map/transpose | solution.py:65
  571.3 14.2 %copy.111 = bf16[8,1,16,1024]{0,1,3,2:T(2,128)(2,1)} copy(bf16[8,1,16,1024]{3,0,2,1:T(8,128)(2,1)S(1)} %fusion.84) | data formatting | bytes 524288 | tf_op jit(solution)/shard_map/convert_element_type | solution.py:141
  585.5 66.0 %fusion.139 = f32[3,3,128,8]{2,3,1,0:T(8,128)S(1)} fusion(bf16[128,1,18,1024]{0,1,3,2:T(2,128)(2,1)} %copy.110, bf16[8,1,16,1024]{0,1,3,2:T(2,128)(2,1)} %copy.111), kind=kOutput, calls=%fused_computation.170 | convolution fusion | flops 301793280 | bytes 5017600 | tf_op jit(solution)/shard_map/transpose | solution.py:65
  651.5 7.7 pad.12
  659.1 17.5 %reshape.183 = bf16[128,18,1,8,129]{4,3,0,1,2:T(8,128)(2,1)} reshape(bf16[128,18,1,1032]{3,0,1,2:T(8,128)(2,1)} %pad.12) | data formatting | bytes 9510912 | tf_op jit(solution)/shard_map/conv_general_dilated | solution.py:45
  676.6 13.1 %copy.103 = bf16[128,18,1,8,129]{0,3,4,1,2:T(8,128)(2,1)} copy(bf16[128,18,1,8,129]{4,3,0,1,2:T(8,128)(2,1)} %reshape.183) | data formatting | bytes 9510912 | tf_op jit(solution)/shard_map/conv_general_dilated | solution.py:45
  690.7 14.4 %broadcast_select_fusion.1 = f32[16,8,129,8]{3,1,2,0:T(8,128)} fusion(pred[8,129]{0,1:T(8,128)(4,1)S(1)} %copy-done.10, bf16[128,18,1,7,2]{0,3,4,1,2:T(8,128)(2,1)S(1)} %slice.86, bf16[128,18,1,8,129]{0,3,4,1,2:T(8,128)(2,1)} %copy.103, bf16[3,3,128,128]{2,3,1,0:T(8,128)(2,1)S(1)} %copy-done.7, s32[]{:T(128)S(6)} %select_n.34), kind=kOutput, calls=%fused_computation.57 | convolution fusion | flops 318968832 | bytes 5644300 | tf_op jit(solution)/shard_map/conv_general_dilated | solution.py:45
  712.9 14.2 %copy.109 = bf16[8,1,16,1024]{0,1,3,2:T(2,128)(2,1)} copy(bf16[8,1,16,1024]{3,0,2,1:T(8,128)(2,1)S(1)} %fusion.101) | data formatting | bytes 524288 | tf_op jit(solution)/shard_map/broadcast_in_dim | solution.py:59
  727.1 66.0 %fusion.138 = f32[3,3,24,8]{2,3,1,0:T(8,128)S(1)} fusion(bf16[24,1,18,1024]{0,1,3,2:T(2,128)(2,1)} %copy.108, bf16[8,1,16,1024]{0,1,3,2:T(2,128)(2,1)} %copy.109), kind=kOutput, calls=%fused_computation.169 | convolution fusion | flops 56586240 | bytes 1153792 | tf_op jit(solution)/shard_map/transpose | solution.py:65
  793.1 43.7 %all-reduce.1 = (f32[3,3,24,8]{2,3,1,0:T(8,128)}, f32[3,3,128,8]{2,3,1,0:T(8,128)}, f32[3,3,8,12]{3,2,1,0:T(8,128)}, f32[8]{0:T(128)}) all-reduce(f32[3,3,24,8]{2,3,1,0:T(8,128)S(1)} %fusion.138, f32[3,3,128,8]{2,3,1,0:T(8,128)S(1)} %fusion.139, ...), channel_id=1, replica_groups=mesh['section'=2,'rows'=8,'chan'=8] {'rows'}, use_global_device_ids=true, to_apply=%region_3.4 | all-reduce | flops 11816 | bytes 94528 | tf_op jit(solution)/shard_map/psum | solution.py:159
  (113 shorter events, 115.3 us)
Async XLA Ops:
  7.2 51.3 %copy-start = (bf16[3,3,12,16]{3,2,1,0:T(8,128)(2,1)S(1)}, bf16[3,3,12,16]{3,2,1,0:T(8,128)(2,1)}, u32[]{:S(2)}) copy-start(bf16[3,3,12,16]{3,2,1,0:T(8,128)(2,1)} %param.14) | copy-start | bytes 10372
  7.2 51.3 %copy-start.10 = (pred[8,129]{0,1:T(8,128)(4,1)S(1)}, pred[8,129]{0,1:T(8,128)(4,1)}, u32[]{:S(2)}) copy-start(pred[8,129]{0,1:T(8,128)(4,1)} %constant.100) | copy-start | bytes 3100
  7.2 391.5 %all-reduce.5.cloned.1.call-start = ((), (), s32[]{:S(2)}) async-start(), calls=%async_computation | async-start | bytes 1572864 | tf_op jit(solution)/shard_map/psum | solution.py:134
  8.5 44.0 %collective-permute-start = (bf16[12,2,1024]{2,1,0:T(2,128)(2,1)S(1)}, bf16[12,2,1024]{2,1,0:T(2,128)(2,1)S(1)}, u32[]{:S(2)}, u32[]{:S(2)}) collective-permute-start(bf16[12,2,1024]{2,1,0:T(2,128)(2,1)S(1)} %get-tuple-element.26), channel_id=1, source_target_pairs={{0,8},{8,16},{16,24},{24,32},{32,40},{40,48},{48,56},{1,9},{9,17},... | collective-permute-start | bytes 147464 | tf_op jit(solution)/shard_map/ppermute | solution.py:22
  13.5 39.0 %collective-permute-start.1 = (bf16[12,2,1024]{2,1,0:T(2,128)(2,1)S(1)}, bf16[12,2,1024]{2,1,0:T(2,128)(2,1)S(1)}, u32[]{:S(2)}, u32[]{:S(2)}) collective-permute-start(bf16[12,2,1024]{2,1,0:T(2,128)(2,1)S(1)} %get-tuple-element.27), channel_id=1, source_target_pairs={{8,0},{16,8},{24,16},{32,24},{40,32},{48,40},{56,48},{9,1},{17,9},... | collective-permute-start | bytes 147464 | tf_op jit(solution)/shard_map/ppermute | solution.py:23
  58.5 7.4 copy-start.12
  70.7 38.6 %copy-start.4 = (f32[12,16,1024]{2,1,0:T(8,128)S(1)}, f32[12,16,1024]{2,1,0:T(8,128)}, u32[]{:S(2)}) copy-start(f32[12,16,1024]{2,1,0:T(8,128)} %param.11) | copy-start | bytes 2359300
  70.7 49.0 %copy-start.8 = (bf16[3,3,24,8]{2,3,1,0:T(8,128)(2,1)S(1)}, bf16[3,3,24,8]{2,3,1,0:T(8,128)(2,1)}, u32[]{:S(2)}) copy-start(bf16[3,3,24,8]{2,3,1,0:T(8,128)(2,1)} %param.16) | copy-start | bytes 10372
  109.3 28.8 %copy-start.3 = (bf16[12,16,1024]{2,1,0:T(8,128)(2,1)}, bf16[12,16,1024]{2,1,0:T(8,128)(2,1)S(1)}, u32[]{:S(2)}) copy-start(bf16[12,16,1024]{2,1,0:T(8,128)(2,1)S(1)} %all_gather.15) | copy-start | bytes 1179652
  111.4 26.7 %collective-permute-start.3 = (bf16[12,2,1024]{2,1,0:T(2,128)(2,1)S(1)}, bf16[12,2,1024]{2,1,0:T(2,128)(2,1)S(1)}, u32[]{:S(2)}, u32[]{:S(2)}) collective-permute-start(bf16[12,2,1024]{2,1,0:T(2,128)(2,1)S(1)} %get-tuple-element.25), channel_id=1, source_target_pairs={{8,0},{16,8},{24,16},{32,24},{40,32},{48,40},{56,48},{9,1},{17,9},... | collective-permute-start | bytes 147464 | tf_op jit(solution)/shard_map/ppermute | solution.py:23
  112.7 25.4 %collective-permute-start.2 = (bf16[12,2,1024]{2,1,0:T(2,128)(2,1)S(1)}, bf16[12,2,1024]{2,1,0:T(2,128)(2,1)S(1)}, u32[]{:S(2)}, u32[]{:S(2)}) collective-permute-start(bf16[12,2,1024]{2,1,0:T(2,128)(2,1)S(1)} %get-tuple-element.24), channel_id=1, source_target_pairs={{0,8},{8,16},{16,24},{24,32},{32,40},{40,48},{48,56},{1,9},{9,17},... | collective-permute-start | bytes 147464 | tf_op jit(solution)/shard_map/ppermute | solution.py:22
  159.7 3.9 copy-start.2
  159.8 3.9 copy-start.9
  183.7 64.6 %collective-permute-start.5 = (bf16[8,1,1024]{2,0,1:T(8,128)(2,1)S(1)}, bf16[8,1,1024]{2,0,1:T(8,128)(2,1)S(1)}, u32[]{:S(2)}, u32[]{:S(2)}) collective-permute-start(bf16[8,1,1024]{2,0,1:T(8,128)(2,1)S(1)} %get-tuple-element.33), channel_id=1, source_target_pairs={{8,0},{16,8},{24,16},{32,24},{40,32},{48,40},{56,48},{9,1},{17,9},... | collective-permute-start | bytes 49160 | tf_op jit(solution)/shard_map/ppermute | solution.py:23
  185.0 63.3 %collective-permute-start.4 = (bf16[8,1,1024]{2,0,1:T(8,128)(2,1)S(1)}, bf16[8,1,1024]{2,0,1:T(8,128)(2,1)S(1)}, u32[]{:S(2)}, u32[]{:S(2)}) collective-permute-start(bf16[8,1,1024]{2,0,1:T(8,128)(2,1)S(1)} %get-tuple-element.32), channel_id=1, source_target_pairs={{0,8},{8,16},{16,24},{24,32},{32,40},{40,48},{48,56},{1,9},{9,17},... | collective-permute-start | bytes 49160 | tf_op jit(solution)/shard_map/ppermute | solution.py:22
  248.3 7.5 copy-start.13
  278.1 373.3 %all-gather.2.cloned.1.call-start = ((), (), s32[]{:S(2)}) async-start(), calls=%async_computation.1 | async-start | bytes 5013504 | tf_op jit(solution)/shard_map/all_gather | solution.py:149
  402.2 17.1 %collective-permute-start.7 = (bf16[12,1,1024]{2,1,0:T(2,128)(2,1)S(1)}, bf16[12,1,1024]{2,1,0:T(2,128)(2,1)S(1)}, u32[]{:S(2)}, u32[]{:S(2)}) collective-permute-start(bf16[12,1,1024]{2,1,0:T(2,128)(2,1)S(1)} %get-tuple-element.23), channel_id=1, source_target_pairs={{8,0},{16,8},{24,16},{32,24},{40,32},{48,40},{56,48},{9,1},{17,9},... | collective-permute-start | bytes 73736 | tf_op jit(solution)/shard_map/ppermute | solution.py:23
  403.5 15.8 %collective-permute-start.6 = (bf16[12,1,1024]{2,1,0:T(2,128)(2,1)S(1)}, bf16[12,1,1024]{2,1,0:T(2,128)(2,1)S(1)}, u32[]{:S(2)}, u32[]{:S(2)}) collective-permute-start(bf16[12,1,1024]{2,1,0:T(2,128)(2,1)S(1)} %get-tuple-element.22), channel_id=1, source_target_pairs={{0,8},{8,16},{16,24},{24,32},{32,40},{40,48},{48,56},{1,9},{9,17},... | collective-permute-start | bytes 73736 | tf_op jit(solution)/shard_map/ppermute | solution.py:22
  449.4 68.4 %collective-permute-start.9 = (bf16[8,1,1024]{2,0,1:T(8,128)(2,1)S(1)}, bf16[8,1,1024]{2,0,1:T(8,128)(2,1)S(1)}, u32[]{:S(2)}, u32[]{:S(2)}) collective-permute-start(bf16[8,1,1024]{2,0,1:T(8,128)(2,1)S(1)} %get-tuple-element.31), channel_id=1, source_target_pairs={{8,0},{16,8},{24,16},{32,24},{40,32},{48,40},{56,48},{9,1},{17,9},... | collective-permute-start | bytes 49160 | tf_op jit(solution)/shard_map/ppermute | solution.py:23
  450.7 67.1 %collective-permute-start.8 = (bf16[8,1,1024]{2,0,1:T(8,128)(2,1)S(1)}, bf16[8,1,1024]{2,0,1:T(8,128)(2,1)S(1)}, u32[]{:S(2)}, u32[]{:S(2)}) collective-permute-start(bf16[8,1,1024]{2,0,1:T(8,128)(2,1)S(1)} %get-tuple-element.30), channel_id=1, source_target_pairs={{0,8},{8,16},{16,24},{24,32},{32,40},{40,48},{48,56},{1,9},{9,17},... | collective-permute-start | bytes 49160 | tf_op jit(solution)/shard_map/ppermute | solution.py:22
  472.1 21.3 %copy-start.6 = (bf16[8,1,18,1024]{3,0,2,1:T(8,128)(2,1)S(1)}, bf16[8,1,18,1024]{3,0,2,1:T(8,128)(2,1)}, u32[]{:S(2)}) copy-start(bf16[8,1,18,1024]{3,0,2,1:T(8,128)(2,1)} %get-tuple-element.28) | copy-start | bytes 884740
  676.6 14.1 %copy-start.7 = (bf16[3,3,128,128]{2,3,1,0:T(8,128)(2,1)S(1)}, bf16[3,3,128,128]{2,3,1,0:T(8,128)(2,1)}, u32[]{:S(2)}) copy-start(bf16[3,3,128,128]{2,3,1,0:T(8,128)(2,1)} %all_gather.19) | copy-start | bytes 884740
  705.0 7.3 copy-start.5
  705.0 7.3 copy-start.11
  727.1 109.7 %copy-start.1 = (bf16[3,3,12,16]{3,2,1,0:T(8,128)(2,1)S(1)}, bf16[3,3,12,16]{3,2,1,0:T(8,128)(2,1)}, u32[]{:S(2)}) copy-start(bf16[3,3,12,16]{3,2,1,0:T(8,128)(2,1)} %param.14) | copy-start | bytes 10372
Sparse Core Ops, SparseCore 0:
  278.3 120.3 all-reduce.4
  518.7 40.0 all-gather.1
where the time goes:
time: 855 us; the launch traced here: 844 us
  matrix products  255 us (30%)
  local copies, waits for them, and re-layouts  251 us (29%)
  blocking collectives  145 us (17%)
  waiting for transfers between devices  111 us (13%)
  starting transfers between devices  38 us (4%)
  other arithmetic  25.3 us (3%)
  between operations  19.2 us (2%)
    transpose x3, matrix products, kernel_grad(): return jnp.transpose(result_conv, (2, 3, 0, 1))  184 us
    conv_general_dilated x28, local copies, waits for them, and re-layouts, conv_rows(): lax.conv_general_dilated(grid_field[None], kernel, (1, 1), ((0, 0), (1, 1...  147 us
    psum x1, waiting for transfers between devices, shards(): out_full = lax.psum(out_part, ('section', 'chan'))  111 us
    conv_general_dilated x7, matrix products, conv_rows(): lax.conv_general_dilated(grid_field[None], kernel, (1, 1), ((0, 0), (1, 1...  70.3 us
    psum x1, blocking collectives, shards(): lax.psum((grad_parts[0], grad_parts[1], grad_parts[2], grad_parts[3]), 'r...  43.7 us
    ppermute x5, starting transfers between devices, padded(): before = lax.ppermute(last, axis, up)  31.5 us
    unnamed x1, blocking collectives  30.4 us
    broadcast_in_dim x3, local copies, waits for them, and re-layouts, kernel_grad(): grid_field[:, None]  29 us
  transfers between devices with their start and end apart: 12, of which 1 were waited for; matrix products, arithmetic and copies ran while one was open for 30% of the time, Pallas kernels for 0%

commit v1 on v0

--- a/solution.py
+++ b/solution.py
@@ -131,7 +131,7 @@
     second_hidden = jax.nn.silu(second_act).astype(jnp.bfloat16)
     second_rim = padded(second_hidden, (("rows", 1),), 1)
     out_part = conv_rows(second_rim, third_kernel)
-    out_full = lax.psum(out_part, ("section", "chan"))
+    out_full = lax.psum(lax.psum(out_part, "chan"), "section")
     den_value = skip_coef * noisy_field + out_coef * out_full
     out_delta = (2.0 * loss_weight * out_coef * grad_scale * (den_value - resid_field)).astype(
         jnp.bfloat16

time: 855 us -> 786 us (0.919)
  waiting for transfers between devices: 111 us -> 42.1 us
    psum x1 -> x2, waiting for transfers between devices: 111 us -> 40.6 us  [shards(): out_full = lax.psum(lax.psum(out_part, 'chan'), 'section')]
  transfers between devices with their start and end apart: 12 -> 13, of which waited for: 1 -> 3; matrix products, arithmetic and copies ran while one was open for 30% -> 33% of each run, Pallas kernels for 0% -> 0%
where the time goes in v1:
time: 786 us; the launch traced here: 775 us
  matrix products  255 us (32%)
  local copies, waits for them, and re-layouts  251 us (32%)
  blocking collectives  145 us (18%)
  waiting for transfers between devices  42.1 us (5%)
  starting transfers between devices  38.5 us (5%)
  other arithmetic  24.4 us (3%)
  between operations  18.9 us (2%)
    transpose x3, matrix products, kernel_grad(): return jnp.transpose(result_conv, (2, 3, 0, 1))  184 us
    conv_general_dilated x28, local copies, waits for them, and re-layouts, conv_rows(): lax.conv_general_dilated(grid_field[None], kernel, (1, 1), ((0, 0), (1, 1...  147 us
    conv_general_dilated x7, matrix products, conv_rows(): lax.conv_general_dilated(grid_field[None], kernel, (1, 1), ((0, 0), (1, 1...  70.5 us
    psum x1, blocking collectives, shards(): lax.psum((grad_parts[0], grad_parts[1], grad_parts[2], grad_parts[3]), 'r...  43.7 us
    psum x2, waiting for transfers between devices, shards(): out_full = lax.psum(lax.psum(out_part, 'chan'), 'section')  40.6 us
    ppermute x5, starting transfers between devices, padded(): before = lax.ppermute(last, axis, up)  31.9 us
    unnamed x1, blocking collectives  30.4 us
    broadcast_in_dim x3, local copies, waits for them, and re-layouts, kernel_grad(): grid_field[:, None]  29 us
  transfers between devices with their start and end apart: 13, of which 3 were waited for; matrix products, arithmetic and copies ran while one was open for 33% of the time, Pallas kernels for 0%

profile of v1, /device:TPU:0, one launch (start us, length us, event | category | flops | bytes accessed | tf_op | source)
XLA Modules:
  0.0 774.9 jit_solution(14521970968733553999)
XLA Ops:
  18.9 30.4 %all-reduce = bf16[128]{0:T(256)(128)(2,1)S(1)} all-reduce(bf16[128]{0:T(256)(128)(2,1)S(1)} %dynamic-update-slice), channel_id=1, replica_groups=mesh['section'=2,'rows'=8,'chan'=8] {'section','chan'}, use_global_device_ids=true, to_apply=%add | all-reduce | flops 128 | bytes 512
  57.3 7.3 select_bitcast_fusion.1
  74.2 27.6 %all-reduce.9 = bf16[12,8,1024]{2,1,0:T(8,128)(2,1)S(1)} all-reduce(f32[12,8,1024]{2,1,0:T(8,128)S(1)} %slice_bitcast_fusion.3), channel_id=1, replica_groups=mesh['section'=2,'rows'=8,'chan'=8] {'chan'}, use_global_device_ids=true, to_apply=%region_1.2 | all-reduce | flops 98304 | bytes 589824 | tf_op jit(solution)/shard_map/psum | solution.py:112
  111.6 7.0 collective-permute-start.2
  118.6 18.4 %all_gather.16 = bf16[3,3,24,128]{2,3,1,0:T(8,128)(2,1)S(1)} all-gather(bf16[3,3,24,8]{2,3,1,0:T(8,128)(2,1)S(1)} %copy-done.8), channel_id=1, replica_groups=mesh['section'=2,'rows'=8,'chan'=8] {'section','chan'}, dimensions={3}, use_global_device_ids=true | all-gather | bytes 58752 | tf_op jit(solution)/shard_map/all_gather | solution.py:121
  149.7 8.9 %broadcast_select_fusion = f32[18,8,129,128]{3,1,2,0:T(8,128)S(1)} fusion(pred[8,129]{0,1:T(8,128)(4,1)S(1)} %copy-done.10, bf16[3,3,24,128]{2,3,1,0:T(8,128)(2,1)S(1)} %all_gather.16, bf16[24,20,1,7,2]{0,3,4,1,2:T(8,128)(2,1)S(1)} %slice.71, bf16[24,20,1,8,129]{0,3,4,1,2:T(8,128)(2,1)} %copy.92), kind=kOutput, calls=%fused_computation.56 | convolution fusion | flops 1032574464 | bytes 10571400 | tf_op jit(solution)/shard_map/conv_general_dilated | solution.py:45
  162.5 12.6 %fusion.30 = f32[16,8,129,8]{3,1,2,0:T(8,128)} fusion(bf16[3,3,128,8]{2,3,1,0:T(8,128)(2,1)S(1)} %copy-done.9, bf16[18,1,7,1,128]{4,2,3,0,1:T(8,128)(2,1)S(1)} %get-tuple-element.17, bf16[18,1,7,1,128]{4,2,3,0,1:T(8,128)(2,1)S(1)} %get-tuple-element.16, bf16[18,1,8,129,128]{4,2,3,0,1:T(8,128)(2,1)S(1)} %select_bitcast_fusion), kind=kOutput, calls=%fused_computation.39 | convolution fusion | flops 328495104 | bytes 5366784 | tf_op jit(solution)/shard_map/conv_general_dilated | solution.py:45
  183.9 7.3 collective-permute-start.4
  200.4 11.2 %broadcast_select_fusion.3 = f32[16,8,129,12]{3,1,2,0:T(8,128)} fusion(pred[8,129]{0,1:T(8,128)(4,1)S(1)} %copy-done.10, bf16[3,3,8,12]{3,2,1,0:T(8,128)(2,1)S(1)} %copy-done.13, bf16[8,18,1,7,2]{0,3,4,1,2:T(8,128)(2,1)S(1)} %slice.77, bf16[8,18,1,8,129]{0,3,4,1,2:T(8,128)(2,1)} %copy.95), kind=kOutput, calls=%fused_computation.59 | convolution fusion | flops 29636352 | bytes 1096584 | tf_op jit(solution)/shard_map/conv_general_dilated | solution.py:45
  211.6 8.1 %copy.96 = f32[16,8,129,12]{2,1,0,3:T(8,128)} copy(f32[16,8,129,12]{3,1,2,0:T(8,128)} %broadcast_select_fusion.3) | data formatting | bytes 1585152 | tf_op jit(solution)/shard_map/conv_general_dilated | solution.py:45
  223.6 18.4 %all_gather.19 = bf16[3,3,128,128]{2,3,1,0:T(8,128)(2,1)} all-gather(bf16[3,3,128,8]{2,3,1,0:T(8,128)(2,1)S(1)} %copy-done.9), channel_id=1, replica_groups=mesh['section'=2,'rows'=8,'chan'=8] {'section','chan'}, dimensions={3}, use_global_device_ids=true | all-gather | bytes 313344 | tf_op jit(solution)/shard_map/all_gather | solution.py:146
  242.5 18.8 %copy.120 = f32[18,8,129,128]{2,1,3,0:T(8,128)} copy(f32[18,8,129,128]{3,1,2,0:T(8,128)} %copy-done.2) | data formatting | bytes 19021824 | tf_op jit(solution)/shard_map/conv_general_dilated | solution.py:45
  261.2 18.0 %reshape.184 = f32[18,1,1032,128]{2,3,0,1:T(8,128)} reshape(f32[18,8,129,128]{2,1,3,0:T(8,128)} %copy.120) | data formatting | bytes 19021824 | tf_op jit(solution)/shard_map/conv_general_dilated | solution.py:45
  286.3 8.2 %select_convert_fusion.1 = bf16[128,1,18,1024]{3,0,2,1:T(8,128)(2,1)} fusion(f32[128]{0:T(128)S(1)} %multiply_add_fusion.3, pred[18]{0:T(512)(128)(4,1)S(1)} %compare_and_fusion, f32[18,1,1032,128]{2,3,0,1:T(8,128)} %reshape.184), kind=kLoop, calls=%fused_computation.14 | loop fusion | flops 16515072 | bytes 14156306 | tf_op jit(solution)/shard_map/convert_element_type | solution.py:126
  295.1 33.7 %all-reduce.8.cloned.1.call-done = f32[12,16,1024]{2,1,0:T(8,128)} async-done(((f32[12,16,1024]{2,1,0:T(8,128)}), f32[12,16,1024]{2,1,0:T(8,128)}) %all-reduce.8.cloned.1.call-update) | async-done | bytes 786448 | tf_op jit(solution)/shard_map/psum | solution.py:134
  340.6 9.3 %slice.88 = f32[18,1,1024,128]{2,3,0,1:T(8,128)} slice(f32[18,1,1032,128]{2,3,0,1:T(8,128)} %reshape.184), slice={[0:18], [0:1], [0:1024], [0:128]} | slice | bytes 18874368 | tf_op jit(solution)/shard_map/conv_general_dilated | solution.py:45
  359.6 11.1 %broadcast_select_fusion.2 = f32[16,8,129,8]{3,1,2,0:T(8,128)} fusion(pred[8,129]{0,1:T(8,128)(4,1)S(1)} %copy-done.10, bf16[3,3,8,12]{3,2,1,0:T(8,128)(2,1)S(1)} %copy-done.13, bf16[12,18,1,7,2]{0,3,4,1,2:T(8,128)(2,1)S(1)} %slice.82, bf16[12,18,1,8,129]{0,3,4,1,2:T(8,128)(2,1)} %copy.99), kind=kOutput, calls=%fused_computation.58 | convolution fusion | flops 30023040 | bytes 983016 | tf_op jit(solution)/shard_map/conv_general_dilated | solution.py:45
  370.7 7.5 copy.100
  389.5 13.0 %copy.108 = bf16[24,1,18,1024]{0,1,3,2:T(2,128)(2,1)} copy(bf16[24,1,18,1024]{3,2,0,1:T(8,128)(2,1)S(1)} %slice_bitcast_fusion) | data formatting | bytes 1769472 | tf_op jit(solution)/shard_map/broadcast_in_dim | solution.py:58
  402.5 21.4 %copy.110 = bf16[128,1,18,1024]{0,1,3,2:T(2,128)(2,1)} copy(bf16[128,1,18,1024]{3,0,2,1:T(8,128)(2,1)} %select_convert_fusion.1) | data formatting | bytes 9437184 | tf_op jit(solution)/shard_map/convert_element_type | solution.py:126
  423.9 15.5 %copy.112 = bf16[8,1,18,1024]{0,1,3,2:T(2,128)(2,1)} copy(bf16[8,1,18,1024]{3,0,2,1:T(8,128)(2,1)S(1)} %copy-done.6) | data formatting | bytes 589824 | tf_op jit(solution)/shard_map/broadcast_in_dim | solution.py:58
  439.5 9.3 %copy.113 = bf16[12,1,16,1024]{0,1,3,2:T(2,128)(2,1)} copy(bf16[12,1,16,1024]{3,2,0,1:T(8,128)(2,1)S(1)} %bitcast.183) | data formatting | bytes 786432 | tf_op jit(solution)/shard_map/broadcast_in_dim | solution.py:59
  449.5 52.5 %fusion.140 = f32[3,3,8,12]{3,2,1,0:T(8,128)S(1)} fusion(bf16[8,1,18,1024]{0,1,3,2:T(2,128)(2,1)} %copy.112, bf16[12,1,16,1024]{0,1,3,2:T(2,128)(2,1)} %copy.113), kind=kOutput, calls=%fused_computation.171 | convolution fusion | flops 28293120 | bytes 691584 | tf_op jit(solution)/shard_map/transpose | solution.py:65
  502.3 14.3 %copy.111 = bf16[8,1,16,1024]{0,1,3,2:T(2,128)(2,1)} copy(bf16[8,1,16,1024]{3,0,2,1:T(8,128)(2,1)S(1)} %fusion.84) | data formatting | bytes 524288 | tf_op jit(solution)/shard_map/convert_element_type | solution.py:141
  516.5 66.0 %fusion.139 = f32[3,3,128,8]{2,3,1,0:T(8,128)S(1)} fusion(bf16[128,1,18,1024]{0,1,3,2:T(2,128)(2,1)} %copy.110, bf16[8,1,16,1024]{0,1,3,2:T(2,128)(2,1)} %copy.111), kind=kOutput, calls=%fused_computation.170 | convolution fusion | flops 301793280 | bytes 5017600 | tf_op jit(solution)/shard_map/transpose | solution.py:65
  582.5 7.7 pad.12
  590.1 17.5 %reshape.183 = bf16[128,18,1,8,129]{4,3,0,1,2:T(8,128)(2,1)} reshape(bf16[128,18,1,1032]{3,0,1,2:T(8,128)(2,1)} %pad.12) | data formatting | bytes 9510912 | tf_op jit(solution)/shard_map/conv_general_dilated | solution.py:45
  607.6 13.1 %copy.103 = bf16[128,18,1,8,129]{0,3,4,1,2:T(8,128)(2,1)} copy(bf16[128,18,1,8,129]{4,3,0,1,2:T(8,128)(2,1)} %reshape.183) | data formatting | bytes 9510912 | tf_op jit(solution)/shard_map/conv_general_dilated | solution.py:45
  621.7 14.4 %broadcast_select_fusion.1 = f32[16,8,129,8]{3,1,2,0:T(8,128)} fusion(pred[8,129]{0,1:T(8,128)(4,1)S(1)} %copy-done.10, bf16[128,18,1,7,2]{0,3,4,1,2:T(8,128)(2,1)S(1)} %slice.86, bf16[128,18,1,8,129]{0,3,4,1,2:T(8,128)(2,1)} %copy.103, bf16[3,3,128,128]{2,3,1,0:T(8,128)(2,1)S(1)} %copy-done.7, s32[]{:T(128)S(6)} %select_n.34), kind=kOutput, calls=%fused_computation.57 | convolution fusion | flops 318968832 | bytes 5644300 | tf_op jit(solution)/shard_map/conv_general_dilated | solution.py:45
  644.0 14.2 %copy.109 = bf16[8,1,16,1024]{0,1,3,2:T(2,128)(2,1)} copy(bf16[8,1,16,1024]{3,0,2,1:T(8,128)(2,1)S(1)} %fusion.101) | data formatting | bytes 524288 | tf_op jit(solution)/shard_map/broadcast_in_dim | solution.py:59
  658.3 66.0 %fusion.138 = f32[3,3,24,8]{2,3,1,0:T(8,128)S(1)} fusion(bf16[24,1,18,1024]{0,1,3,2:T(2,128)(2,1)} %copy.108, bf16[8,1,16,1024]{0,1,3,2:T(2,128)(2,1)} %copy.109), kind=kOutput, calls=%fused_computation.169 | convolution fusion | flops 56586240 | bytes 1153792 | tf_op jit(solution)/shard_map/transpose | solution.py:65
  724.3 43.7 %all-reduce.1 = (f32[3,3,24,8]{2,3,1,0:T(8,128)}, f32[3,3,128,8]{2,3,1,0:T(8,128)}, f32[3,3,8,12]{3,2,1,0:T(8,128)}, f32[8]{0:T(128)}) all-reduce(f32[3,3,24,8]{2,3,1,0:T(8,128)S(1)} %fusion.138, f32[3,3,128,8]{2,3,1,0:T(8,128)S(1)} %fusion.139, ...), channel_id=1, replica_groups=mesh['section'=2,'rows'=8,'chan'=8] {'rows'}, use_global_device_ids=true, to_apply=%region_4.5 | all-reduce | flops 11816 | bytes 94528 | tf_op jit(solution)/shard_map/psum | solution.py:159
  (118 shorter events, 123.7 us)
Async XLA Ops:
  7.2 50.1 %copy-start = (bf16[3,3,12,16]{3,2,1,0:T(8,128)(2,1)S(1)}, bf16[3,3,12,16]{3,2,1,0:T(8,128)(2,1)}, u32[]{:S(2)}) copy-start(bf16[3,3,12,16]{3,2,1,0:T(8,128)(2,1)} %param.14) | copy-start | bytes 10372
  7.2 50.1 %copy-start.10 = (pred[8,129]{0,1:T(8,128)(4,1)S(1)}, pred[8,129]{0,1:T(8,128)(4,1)}, u32[]{:S(2)}) copy-start(pred[8,129]{0,1:T(8,128)(4,1)} %constant.100) | copy-start | bytes 3100
  7.2 279.0 %all-reduce.6.cloned.1.call-start = ((), (), s32[]{:S(2)}) async-start(), calls=%async_computation | async-start | bytes 1572864 | tf_op jit(solution)/shard_map/psum | solution.py:134
  8.5 42.8 %collective-permute-start = (bf16[12,2,1024]{2,1,0:T(2,128)(2,1)S(1)}, bf16[12,2,1024]{2,1,0:T(2,128)(2,1)S(1)}, u32[]{:S(2)}, u32[]{:S(2)}) collective-permute-start(bf16[12,2,1024]{2,1,0:T(2,128)(2,1)S(1)} %get-tuple-element.26), channel_id=1, source_target_pairs={{0,8},{8,16},{16,24},{24,32},{32,40},{40,48},{48,56},{1,9},{9,17},... | collective-permute-start | bytes 147464 | tf_op jit(solution)/shard_map/ppermute | solution.py:22
  13.5 37.8 %collective-permute-start.1 = (bf16[12,2,1024]{2,1,0:T(2,128)(2,1)S(1)}, bf16[12,2,1024]{2,1,0:T(2,128)(2,1)S(1)}, u32[]{:S(2)}, u32[]{:S(2)}) collective-permute-start(bf16[12,2,1024]{2,1,0:T(2,128)(2,1)S(1)} %get-tuple-element.27), channel_id=1, source_target_pairs={{8,0},{16,8},{24,16},{32,24},{40,32},{48,40},{56,48},{9,1},{17,9},... | collective-permute-start | bytes 147464 | tf_op jit(solution)/shard_map/ppermute | solution.py:23
  57.3 7.4 copy-start.12
  69.6 38.6 %copy-start.4 = (f32[12,16,1024]{2,1,0:T(8,128)S(1)}, f32[12,16,1024]{2,1,0:T(8,128)}, u32[]{:S(2)}) copy-start(f32[12,16,1024]{2,1,0:T(8,128)} %param.11) | copy-start | bytes 2359300
  69.6 49.0 %copy-start.8 = (bf16[3,3,24,8]{2,3,1,0:T(8,128)(2,1)S(1)}, bf16[3,3,24,8]{2,3,1,0:T(8,128)(2,1)}, u32[]{:S(2)}) copy-start(bf16[3,3,24,8]{2,3,1,0:T(8,128)(2,1)} %param.16) | copy-start | bytes 10372
  108.2 28.8 %copy-start.3 = (bf16[12,16,1024]{2,1,0:T(8,128)(2,1)}, bf16[12,16,1024]{2,1,0:T(8,128)(2,1)S(1)}, u32[]{:S(2)}) copy-start(bf16[12,16,1024]{2,1,0:T(8,128)(2,1)S(1)} %all_gather.15) | copy-start | bytes 1179652
  110.3 26.7 %collective-permute-start.3 = (bf16[12,2,1024]{2,1,0:T(2,128)(2,1)S(1)}, bf16[12,2,1024]{2,1,0:T(2,128)(2,1)S(1)}, u32[]{:S(2)}, u32[]{:S(2)}) collective-permute-start(bf16[12,2,1024]{2,1,0:T(2,128)(2,1)S(1)} %get-tuple-element.25), channel_id=1, source_target_pairs={{8,0},{16,8},{24,16},{32,24},{40,32},{48,40},{56,48},{9,1},{17,9},... | collective-permute-start | bytes 147464 | tf_op jit(solution)/shard_map/ppermute | solution.py:23
  111.6 25.4 %collective-permute-start.2 = (bf16[12,2,1024]{2,1,0:T(2,128)(2,1)S(1)}, bf16[12,2,1024]{2,1,0:T(2,128)(2,1)S(1)}, u32[]{:S(2)}, u32[]{:S(2)}) collective-permute-start(bf16[12,2,1024]{2,1,0:T(2,128)(2,1)S(1)} %get-tuple-element.24), channel_id=1, source_target_pairs={{0,8},{8,16},{16,24},{24,32},{32,40},{40,48},{48,56},{1,9},{9,17},... | collective-permute-start | bytes 147464 | tf_op jit(solution)/shard_map/ppermute | solution.py:22
  158.6 3.9 copy-start.2
  158.6 3.9 copy-start.9
  182.0 18.4 %copy-start.13 = (bf16[3,3,8,12]{3,2,1,0:T(8,128)(2,1)S(1)}, bf16[3,3,8,12]{3,2,1,0:T(8,128)(2,1)}, u32[]{:S(2)}) copy-start(bf16[3,3,8,12]{3,2,1,0:T(8,128)(2,1)} %param.18) | copy-start | bytes 5188
  182.6 8.6 %collective-permute-start.5 = (bf16[8,1,1024]{2,0,1:T(8,128)(2,1)S(1)}, bf16[8,1,1024]{2,0,1:T(8,128)(2,1)S(1)}, u32[]{:S(2)}, u32[]{:S(2)}) collective-permute-start(bf16[8,1,1024]{2,0,1:T(8,128)(2,1)S(1)} %get-tuple-element.33), channel_id=1, source_target_pairs={{8,0},{16,8},{24,16},{32,24},{40,32},{48,40},{56,48},{9,1},{17,9},... | collective-permute-start | bytes 49160 | tf_op jit(solution)/shard_map/ppermute | solution.py:23
  183.9 8.7 %collective-permute-start.4 = (bf16[8,1,1024]{2,0,1:T(8,128)(2,1)S(1)}, bf16[8,1,1024]{2,0,1:T(8,128)(2,1)S(1)}, u32[]{:S(2)}, u32[]{:S(2)}) collective-permute-start(bf16[8,1,1024]{2,0,1:T(8,128)(2,1)S(1)} %get-tuple-element.32), channel_id=1, source_target_pairs={{0,8},{8,16},{16,24},{24,32},{32,40},{40,48},{48,56},{1,9},{9,17},... | collective-permute-start | bytes 49160 | tf_op jit(solution)/shard_map/ppermute | solution.py:22
  219.6 22.3 %copy-start.14 = (bf16[8]{0:T(256)(128)(2,1)S(1)}, bf16[8]{0:T(256)(128)(2,1)}, u32[]{:S(2)}) copy-start(bf16[8]{0:T(256)(128)(2,1)} %param.19) | copy-start | bytes 52
  222.7 106.1 %all-reduce.8.cloned.1.call-start = ((), (), s32[]{:S(2)}) async-start(), calls=%async_computation.1 | async-start | bytes 1572864 | tf_op jit(solution)/shard_map/psum | solution.py:134
  286.2 296.3 %all-gather.2.cloned.1.call-start = ((), (), s32[]{:S(2)}) async-start(), calls=%async_computation.2 | async-start | bytes 5013504 | tf_op jit(solution)/shard_map/all_gather | solution.py:149
  332.3 17.5 %collective-permute-start.7 = (bf16[12,1,1024]{2,1,0:T(2,128)(2,1)S(1)}, bf16[12,1,1024]{2,1,0:T(2,128)(2,1)S(1)}, u32[]{:S(2)}, u32[]{:S(2)}) collective-permute-start(bf16[12,1,1024]{2,1,0:T(2,128)(2,1)S(1)} %get-tuple-element.23), channel_id=1, source_target_pairs={{8,0},{16,8},{24,16},{32,24},{40,32},{48,40},{56,48},{9,1},{17,9},... | collective-permute-start | bytes 73736 | tf_op jit(solution)/shard_map/ppermute | solution.py:23
  333.6 16.2 %collective-permute-start.6 = (bf16[12,1,1024]{2,1,0:T(2,128)(2,1)S(1)}, bf16[12,1,1024]{2,1,0:T(2,128)(2,1)S(1)}, u32[]{:S(2)}, u32[]{:S(2)}) collective-permute-start(bf16[12,1,1024]{2,1,0:T(2,128)(2,1)S(1)} %get-tuple-element.22), channel_id=1, source_target_pairs={{0,8},{8,16},{16,24},{24,32},{32,40},{40,48},{48,56},{1,9},{9,17},... | collective-permute-start | bytes 73736 | tf_op jit(solution)/shard_map/ppermute | solution.py:22
  380.1 68.7 %collective-permute-start.9 = (bf16[8,1,1024]{2,0,1:T(8,128)(2,1)S(1)}, bf16[8,1,1024]{2,0,1:T(8,128)(2,1)S(1)}, u32[]{:S(2)}, u32[]{:S(2)}) collective-permute-start(bf16[8,1,1024]{2,0,1:T(8,128)(2,1)S(1)} %get-tuple-element.31), channel_id=1, source_target_pairs={{8,0},{16,8},{24,16},{32,24},{40,32},{48,40},{56,48},{9,1},{17,9},... | collective-permute-start | bytes 49160 | tf_op jit(solution)/shard_map/ppermute | solution.py:23
  381.4 67.4 %collective-permute-start.8 = (bf16[8,1,1024]{2,0,1:T(8,128)(2,1)S(1)}, bf16[8,1,1024]{2,0,1:T(8,128)(2,1)S(1)}, u32[]{:S(2)}, u32[]{:S(2)}) collective-permute-start(bf16[8,1,1024]{2,0,1:T(8,128)(2,1)S(1)} %get-tuple-element.30), channel_id=1, source_target_pairs={{0,8},{8,16},{16,24},{24,32},{32,40},{40,48},{48,56},{1,9},{9,17},... | collective-permute-start | bytes 49160 | tf_op jit(solution)/shard_map/ppermute | solution.py:22
  402.5 21.4 %copy-start.6 = (bf16[8,1,18,1024]{3,0,2,1:T(8,128)(2,1)S(1)}, bf16[8,1,18,1024]{3,0,2,1:T(8,128)(2,1)}, u32[]{:S(2)}) copy-start(bf16[8,1,18,1024]{3,0,2,1:T(8,128)(2,1)} %get-tuple-element.28) | copy-start | bytes 884740
  607.6 14.1 %copy-start.7 = (bf16[3,3,128,128]{2,3,1,0:T(8,128)(2,1)S(1)}, bf16[3,3,128,128]{2,3,1,0:T(8,128)(2,1)}, u32[]{:S(2)}) copy-start(bf16[3,3,128,128]{2,3,1,0:T(8,128)(2,1)} %all_gather.19) | copy-start | bytes 884740
  636.1 7.3 copy-start.5
  636.1 7.3 copy-start.11
  658.2 109.7 %copy-start.1 = (bf16[3,3,12,16]{3,2,1,0:T(8,128)(2,1)S(1)}, bf16[3,3,12,16]{3,2,1,0:T(8,128)(2,1)}, u32[]{:S(2)}) copy-start(bf16[3,3,12,16]{3,2,1,0:T(8,128)(2,1)} %param.14) | copy-start | bytes 10372
Sparse Core Ops, SparseCore 0:
  222.9 63.2 all-reduce.5
  288.8 39.9 all-reduce.7
  449.7 41.1 all-gather.1
